TPU v7x, 256 devices: a whole 4x4x8 slice. The times are simulated.
256 devices in a mesh: dp: 16 (over z_hi, y, core), ctx: 16 (over z_lo, x).
Axes of the slice: x: 4, y: 4, z: 8 (z_hi: 2, z_lo: 4; z = z_hi * 4 + z_lo), core: 2. Of those that a mesh axis runs over, the one named last changes fastest.
Arguments:
- q_self: bfloat16 [16, 2048, 2048], P('dp', 'ctx'), may hold values from -128 to 128
- k_self: bfloat16 [16, 2048, 2048], P('dp', 'ctx'), may hold values from -10 to 10
- v_self: bfloat16 [16, 2048, 2048], P('dp', 'ctx'), may hold values from -6 to 6
- q_cross: bfloat16 [16, 2048, 2048], P('dp', 'ctx'), may hold values from -128 to 128
- db_keys: bfloat16 [32, 128, 2048], P('dp'), may hold values from -10 to 10
- db_values: bfloat16 [32, 128, 2048], P('dp'), may hold values from -6 to 6
- nb_shard: int32 [16, 32, 2], P('dp', 'ctx'), may hold values from 0 to 15, as said below
- nb_row: int32 [16, 32, 2], P('dp', 'ctx'), may hold values from 0 to 1
Outputs:
- mixed: bfloat16 [16, 2048, 2048], P('dp', 'ctx')
Inputs may be any that keep to these rules, and one draw needn't show every extreme that they name: `nb_shard`: at most 1 of the neighbours of the groups of one device lie on one shard, and some shard holds exactly 1 of them.
All inputs are finite; a program needn't handle non-finite values.
Results may differ from a plain program's by a relative error of at most 0.0045.
Values may be sent and summed in bfloat16 or wider, within the bound.
A program may use at most 128 MiB of HBM per device.

v0:
```python
import jax
import jax.numpy as jnp
from jax import lax
from jax.experimental import pallas as pl
from jax.experimental.pallas import tpu as pltpu
from jax.sharding import PartitionSpec as P

HEADS = 16
HD = 128
GROUP = 64
NEIGH = 2
NLEN = 128
TOK = 128
DB_DEV = 2
N_DP = 16
HALF = 8
XS = 4
LOCAL = HEADS // XS
WIDE = LOCAL * HD
ROWS = 256
PER = ROWS // TOK
QB = XS // PER
EXPO = HD**-0.5 * 1.4426950408889634
MESH = pl.DeviceIdType.MESH
NT = (((1,), (1,)), ((), ()))
NN = (((1,), (0,)), ((), ()))
QC, KS, VS, QS, OUT = range(5)
ZK, ZV, ZQ2, ZQ3, ZQ3B, ZO2, ZS2, ZO3, ZS3, ZO3B, ZS3B = range(11)


def cols(head):
    return pl.ds(pl.multiple_of(head * HD, HD), HD)


def kernel(
    qs_ref, ks_ref, vs_ref, qc_ref, kd_ref, vd_ref, shard_ref, row_ref, out_ref,
    qs, ks, vs, qc, k0, v0, q2, q3, kd, vd, idx, idx_s, cross, scores, tops, totals, accs,
    part_out, stat_out, part_in, stat_in, mixed, cross_out, kf, vf,
    x_send, x_recv, qc_send, qc_recv, idx_send, idx_recv, back_send, back_recv, z_send, z_recv,
    far_send, far_recv, y_send, core_send, db_recv, own_sem, db_own, number_sem, ready,
):
    dp = lax.axis_index("dp")
    me = lax.axis_index("ctx")
    row = me // XS
    x = lax.rem(me, XS)
    near = lax.rem(dp, HALF)
    side = dp - near
    away = HALF - side
    y = near // 2
    core = lax.rem(near, 2)
    other_core = dp + 1 - 2 * core
    far_dp = away + near
    far_ctx = (3 - row) * XS + x
    edge = (row == 0) | (row == 3)
    first_side = dp < HALF
    inner = (row == 1) | (row == 2)
    pair = row + 1 - 2 * lax.rem(row, 2)
    cross_row = jnp.where(inner, pair, row)
    cross_part = jnp.where(inner, 1, 0)

    def x_at(k):
        return lax.rem(x + k, XS)

    def y_at(home, k):
        return home + lax.rem(near + 2 * k, HALF)

    def loop(first, last, body):
        def step(k, carry):
            body(k)
            return carry

        lax.fori_loop(first, last, step, 0)

    barrier = pltpu.get_barrier_semaphore()

    def greet(dp_of, ctx_of):
        pl.semaphore_signal(barrier, inc=1, device_id={"dp": dp_of, "ctx": ctx_of}, device_id_type=MESH)

    def plane(k):
        return lax.rem(y + k // XS, 4), x_at(lax.rem(k, XS))

    def greet_plane(of_row):
        def step(k):
            to_y, to_x = plane(k)
            greet(side + 2 * to_y + core, of_row * XS + to_x)

        return step

    loop(1, jnp.where(edge, 4 * XS, XS), greet_plane(row))
    loop(1, 4 * XS, greet_plane(pair))
    for k in range(1, 4):
        greet(dp, lax.rem(row + k, 4) * XS + x)

    @pl.when(edge)
    def _():
        greet(other_core, me)

    @pl.when(edge & first_side)
    def _():
        greet(far_dp, far_ctx)

    lane = lax.broadcasted_iota(jnp.int32, (8, 128), 1)
    tile = jnp.zeros((8, 128), jnp.int32)
    for g in range(TOK // GROUP):
        for n in range(NEIGH):
            block = shard_ref[0, g, n] * DB_DEV + row_ref[0, g, n]
            tile = jnp.where(lane == g * NEIGH + n, block, tile)
    idx[cross_part, y, x] = tile

    arrays = {KS: (ks_ref, ks), VS: (vs_ref, vs), QS: (qs_ref, qs)}
    blocks = ((kd_ref, kd, kf), (vd_ref, vd, vf))
    wide = pl.ds(pl.multiple_of(x * WIDE, WIDE), WIDE)
    head = x * LOCAL + y

    def own_copy(kind, h):
        arg, buf = arrays[kind]
        return pltpu.make_async_copy(arg.at[:, cols(x * LOCAL + h)], buf.at[h, x], own_sem.at[kind, h])

    def own_qc():
        return pltpu.make_async_copy(qc_ref.at[:, cols(head)], qc.at[0, y, x], own_sem.at[QC, 0])

    def own_db(kind):
        arg, buf, far = blocks[kind]
        return pltpu.make_async_copy(arg.at[:, :, cols(head)], buf.at[pl.ds(dp * DB_DEV, DB_DEV)], db_own.at[kind])

    def own_far(kind):
        arg, buf, far = blocks[kind]
        return pltpu.make_async_copy(far.at[:, :, cols(y)], buf.at[pl.ds(far_dp * DB_DEV, DB_DEV)], db_own.at[2 + kind])

    def start_own(h):
        for kind in (KS, VS, QS):
            own_copy(kind, h).start()

    loop(0, LOCAL, start_own)

    @pl.when(edge)
    def _():
        own_qc().start()
        for kind in range(2):
            own_db(kind).start()

    pl.semaphore_wait(barrier, 21 + jnp.where(edge, 13, 0) + jnp.where(edge & (dp >= HALF), 1, 0))

    @pl.when(edge & (dp >= HALF))
    def _():
        pl.semaphore_signal(ready, inc=1, device_id={"dp": far_dp, "ctx": far_ctx}, device_id_type=MESH)

    def far_copy(kind):
        arg, buf, far = blocks[kind]
        return pltpu.make_async_remote_copy(
            arg.at[:, :, wide], far, far_send.at[kind], far_recv.at[kind],
            device_id={"dp": far_dp, "ctx": far_ctx}, device_id_type=MESH,
        )

    def shard_copy(kind, shard, src, send, target):
        part = blocks[kind][1].at[pl.ds(shard * DB_DEV, DB_DEV)]
        return pltpu.make_async_remote_copy(
            part if src is None else src, part, send, db_recv.at[kind, shard],
            device_id={"dp": target, "ctx": me}, device_id_type=MESH,
        )

    def y_copy(kind, far, k):
        to_y = lax.rem(y + k, 4)
        src = blocks[kind][2].at[:, :, cols(to_y)] if far else blocks[kind][0].at[:, :, cols(x * LOCAL + to_y)]
        return shard_copy(kind, far_dp if far else dp, src, y_send.at[kind, far, k], y_at(side, k))

    def core_pass(kind, far, k):
        src = None
        if k == 0:
            src = blocks[kind][2].at[:, :, cols(y)] if far else blocks[kind][0].at[:, :, cols(head)]
        return shard_copy(kind, y_at(away if far else side, k), src, core_send.at[kind, far, k], other_core)

    def wait_shard(kind, shard):
        shard_copy(kind, shard, None, far_send.at[kind], other_core).wait_recv()

    def qc_copy(k):
        to_y, to_x = plane(k)
        return pltpu.make_async_remote_copy(
            qc_ref.at[:, cols(to_x * LOCAL + to_y)], qc.at[cross_part, y, x], qc_send.at[k], qc_recv.at[cross_part, y, x],
            device_id={"dp": side + 2 * to_y + core, "ctx": cross_row * XS + to_x}, device_id_type=MESH,
        )

    def idx_copy(k):
        to_y, to_x = plane(k)
        return pltpu.make_async_remote_copy(
            idx.at[cross_part, y, x], idx.at[cross_part, y, x], idx_send.at[k], idx_recv.at[cross_part, y, x],
            device_id={"dp": side + 2 * to_y + core, "ctx": cross_row * XS + to_x}, device_id_type=MESH,
        )

    def wait_plane(part):
        def step(k):
            from_y, from_x = plane(k)
            for buf, sent, received in ((idx, idx_send, idx_recv), (qc, qc_send, qc_recv)):
                there = buf.at[part, from_y, from_x]
                pltpu.make_async_remote_copy(
                    there, there, sent.at[k], received.at[part, from_y, from_x],
                    device_id={"dp": side + 2 * from_y + core, "ctx": jnp.where(part == 1, pair, row) * XS + from_x},
                    device_id_type=MESH,
                ).wait_recv()

        return step

    def back_copy(part, k):
        to_y = lax.rem(y + k, 4)
        return pltpu.make_async_remote_copy(
            cross_out.at[part, to_y], cross.at[y], back_send.at[part, k], back_recv.at[y],
            device_id={"dp": y_at(side, k), "ctx": jnp.where(part == 1, pair, row) * XS + x}, device_id_type=MESH,
        )

    def own_back():
        return pltpu.make_async_copy(cross_out.at[0, y], cross.at[y], own_sem.at[QC, 1])

    def x_copy(kind, h, to):
        arg, buf = arrays[kind]
        return pltpu.make_async_remote_copy(
            arg.at[:, cols(to * LOCAL + h)], buf.at[h, x], x_send.at[kind, h, to], x_recv.at[kind, h, x],
            device_id={"dp": dp, "ctx": row * XS + to}, device_id_type=MESH,
        )

    def arrived(kind, h):
        own_copy(kind, h).wait()
        for k in range(1, XS):
            source = x_at(k)
            buf = arrays[kind][1].at[h, source]
            pltpu.make_async_remote_copy(
                buf, buf, x_send.at[kind, h, source], x_recv.at[kind, h, source],
                device_id={"dp": dp, "ctx": row * XS + source}, device_id_type=MESH,
            ).wait_recv()

    def start_x(kinds):
        def step(h):
            for k in (1, 3, 2):
                for kind in kinds:
                    x_copy(kind, h, x_at(k)).start()

        loop(0, LOCAL, step)

    first_plane = jnp.where(inner, 0, 1)

    def start_plane():
        def step(k):
            idx_copy(k).start()
            qc_copy(k).start()

        loop(first_plane, 4 * XS, step)

    def start_near():
        for kind in range(2):
            for k in (1, 3, 2):
                y_copy(kind, 0, k).start()
            core_pass(kind, 0, 0).start()

    def start_far_first():
        @pl.when(dp >= HALF)
        def _():
            for kind in range(2):
                far_copy(kind).start()

    def start_far_second():
        @pl.when(first_side)
        def _():
            pl.semaphore_wait(ready, 1)
            for kind in range(2):
                far_copy(kind).start()

    @pl.when(row == 0)
    def _():
        start_far_first()
        start_x((KS, VS))
        start_near()
        start_plane()
        start_far_second()
        start_x((QS,))

    @pl.when(row == 1)
    def _():
        start_plane()
        start_x((KS, VS))
        start_x((QS,))

    @pl.when(row == 2)
    def _():
        start_x((QS,))
        start_plane()
        start_x((KS, VS))

    @pl.when(row == 3)
    def _():
        start_far_first()
        start_x((QS,))
        start_near()
        start_plane()
        start_far_second()
        start_x((KS, VS))

    def z_copy(kind, h):
        src, dst, to = {
            ZK: (ks.at[h], k0.at[h], 1),
            ZV: (vs.at[h], v0.at[h], 1),
            ZQ2: (qs.at[h], q2.at[h], 1),
            ZQ3: (qs.at[h], q3.at[h], 1),
            ZQ3B: (qs.at[h], q3.at[h], 2),
            ZO2: (part_out.at[0, h], part_in.at[0, h], 2),
            ZS2: (stat_out.at[0, h], stat_in.at[0, h], 2),
            ZO3: (part_out.at[1, h], part_in.at[0, h], 3),
            ZS3: (stat_out.at[1, h], stat_in.at[0, h], 3),
            ZO3B: (part_out.at[1, h], part_in.at[1, h], 3),
            ZS3B: (stat_out.at[1, h], stat_in.at[1, h], 3),
        }[kind]
        return pltpu.make_async_remote_copy(
            src, dst, z_send.at[kind, h], z_recv.at[kind, h],
            device_id={"dp": dp, "ctx": to * XS + x}, device_id_type=MESH,
        )

    def relay(h):
        @pl.when(row == 0)
        def _():
            arrived(KS, h)
            z_copy(ZK, h).start()
            arrived(VS, h)
            z_copy(ZV, h).start()

        @pl.when(row == 2)
        def _():
            arrived(QS, h)
            z_copy(ZQ2, h).start()

        @pl.when(row == 3)
        def _():
            arrived(QS, h)
            z_copy(ZQ3, h).start()
            z_copy(ZQ3B, h).start()

    def far_stage():
        for kind in range(2):
            far_copy(kind).wait_recv()
            for k in (1, 3, 2):
                y_copy(kind, 1, k).start()
            core_pass(kind, 1, 0).start()
            own_far(kind).start()

    def core_stage():
        for far in range(2):
            for kind in range(2):
                for k in (1, 3, 2):
                    wait_shard(kind, y_at(away if far else side, k))
                    core_pass(kind, far, k).start()

    diagonal = lax.broadcasted_iota(jnp.int32, (ROWS, ROWS), 0) >= lax.broadcasted_iota(jnp.int32, (ROWS, ROWS), 1)
    eye = lax.broadcasted_iota(jnp.int32, (TOK, TOK), 0) == lax.broadcasted_iota(jnp.int32, (TOK, TOK), 1)

    def score_block(queries, h, b, chunks, slot):
        q = queries[h, pl.ds(b * PER, PER)].reshape(ROWS, HD)
        peak = None
        for j, (keys, values, c, masked) in enumerate(chunks):
            k = keys[h, pl.ds(c * PER, PER)].reshape(ROWS, HD)
            s = lax.dot_general(q, k, NT, preferred_element_type=jnp.float32)
            if masked:
                s = jnp.where(diagonal, s, -1e30)
            scores[slot, j] = s
            folded = jnp.maximum(s[:, :HD], s[:, HD:])
            peak = folded if peak is None else jnp.maximum(peak, folded)
        return jnp.max(peak, axis=1, keepdims=True)

    def weigh_block(h, chunks, slot, top):
        total = jnp.zeros((ROWS, HD), jnp.float32)
        acc = jnp.zeros((ROWS, HD), jnp.float32)
        for j, (keys, values, c, masked) in enumerate(chunks):
            w = jnp.exp2((scores[slot, j] - top) * EXPO)
            total = total + (w[:, :HD] + w[:, HD:])
            v = values[h, pl.ds(c * PER, PER)].reshape(ROWS, HD)
            acc = acc + lax.dot_general(w.astype(jnp.bfloat16), v, NN, preferred_element_type=jnp.float32)
        return jnp.sum(total, axis=1, keepdims=True), acc

    def attend(h, jobs):
        tops_of = []
        for n in range(len(jobs) + 1):
            if n < len(jobs):
                queries, b, chunks, done = jobs[n]
                tops_of.append(score_block(queries, h, b, chunks, n % 3))
            if n >= 1:
                queries, b, chunks, done = jobs[n - 1]
                done(b, tops_of[n - 1], *weigh_block(h, chunks, (n - 1) % 3, tops_of[n - 1]))

    def partial(queries, h, chunks, place):
        def done(b, top, total, acc):
            part_out[place, h, pl.ds(b * PER, PER)] = (acc / total).astype(jnp.bfloat16).reshape(PER, TOK, HD)
            for p in range(PER):
                rows = slice(p * TOK, (p + 1) * TOK)
                at = b * PER + p
                stat_out[place, h, at : at + 1] = jnp.sum(jnp.where(eye, top[rows], 0.0), axis=0, keepdims=True)
                stat_out[place, h, XS + at : XS + at + 1] = jnp.sum(jnp.where(eye, total[rows], 0.0), axis=0, keepdims=True)

        return [(queries, b, chunks, done) for b in range(QB)]

    def own_rows(h, extra, final):
        def done(b, top, total, acc):
            at = h * QB + b
            if final:
                accs[at] = acc / total
            else:
                accs[at] = acc
                tops[at] = jnp.broadcast_to(top, (ROWS, HD))
                totals[at] = jnp.broadcast_to(total, (ROWS, HD))

        return [(qs, b, extra + [(ks, vs, c, c == b) for c in range(b + 1)], done) for b in range(QB)]

    whole_own = [(ks, vs, c, False) for c in range(QB)]
    whole_first = [(k0, v0, c, False) for c in range(QB)]

    def between(h):
        @pl.when(row == 1)
        def _():
            arrived(KS, h)
            arrived(VS, h)
            z_copy(ZK, h).wait_recv()
            z_copy(ZV, h).wait_recv()
            z_copy(ZQ2, h).wait_recv()
            z_copy(ZQ3, h).wait_recv()
            attend(h, partial(q2, h, whole_first + whole_own, 0) + partial(q3, h, whole_first + whole_own, 1))
            z_copy(ZO2, h).start()
            z_copy(ZS2, h).start()
            z_copy(ZO3, h).start()
            z_copy(ZS3, h).start()

        @pl.when(row == 2)
        def _():
            arrived(KS, h)
            arrived(VS, h)
            z_copy(ZQ3B, h).wait_recv()
            attend(h, partial(q3, h, whole_own, 1))
            z_copy(ZO3B, h).start()
            z_copy(ZS3B, h).start()

    def own_others(h):
        @pl.when(row == 0)
        def _():
            arrived(QS, h)
            attend(h, own_rows(h, [], True))

        @pl.when(row == 1)
        def _():
            arrived(QS, h)
            attend(h, own_rows(h, whole_first, True))

        @pl.when(row == 2)
        def _():
            attend(h, own_rows(h, [], False))

        @pl.when(row == 3)
        def _():
            arrived(KS, h)
            arrived(VS, h)
            attend(h, own_rows(h, [], False))

    def cross_document(part, k):
        doc = lax.rem(y + k, 4)
        groups = [(t, g) for t in range(XS) for g in range(TOK // GROUP)]
        picks = [[idx_s[part, doc, t, 0, g * NEIGH + n] for n in range(NEIGH)] for t, g in groups]
        s = []
        for (t, g), pick in zip(groups, picks):
            keys = jnp.concatenate([kd[block] for block in pick], axis=0)
            q = qc[part, doc, t, pl.ds(g * GROUP, GROUP), :]
            s.append(lax.dot_general(q, keys, NT, preferred_element_type=jnp.float32))
        top = [jnp.max(one, axis=1, keepdims=True) for one in s]
        w = [jnp.exp2((one - high) * EXPO) for one, high in zip(s, top)]
        total = [jnp.sum(one, axis=1, keepdims=True) for one in w]
        o = []
        for one, pick in zip(w, picks):
            values = jnp.concatenate([vd[block] for block in pick], axis=0)
            o.append(lax.dot_general(one.astype(jnp.bfloat16), values, NN, preferred_element_type=jnp.float32))
        for (t, g), one, whole in zip(groups, o, total):
            cross_out[part, doc, t, pl.ds(g * GROUP, GROUP), :] = (one / whole).astype(jnp.bfloat16)

        here = (part == 0) & (k == 0)

        @pl.when(jnp.logical_not(here))
        def _():
            back_copy(part, k).start()

        @pl.when(here)
        def _():
            own_back().start()

    def cross_stage():
        own_qc().wait()
        for kind in range(2):
            own_db(kind).wait()
            own_far(kind).wait()

        def wait_other_core(k):
            for kind in range(2):
                wait_shard(kind, 2 * k + 1 - core)

        loop(0, HALF, wait_other_core)

        def cross_row_of(n):
            part = 1 - n
            loop(n, 4 * XS, wait_plane(part))
            numbers = pltpu.make_async_copy(idx.at[part], idx_s.at[part], number_sem)
            numbers.start()
            numbers.wait()
            loop(0, 4, lambda k: cross_document(part, 3 - k))

        loop(0, 2, cross_row_of)

    @pl.when(row == 0)
    def _():
        relay(0)
        relay(1)
        far_stage()
        relay(2)
        relay(3)

    @pl.when(row >= 2)
    def _():
        loop(0, LOCAL, relay)

    pl.when(row == 3)(far_stage)

    @pl.when(edge)
    def _():
        core_stage()
        cross_stage()

    loop(0, LOCAL, between)

    def merge(h, parts):
        for b in range(QB):
            at = h * QB + b
            for p in range(PER):
                rows = slice(p * TOK, (p + 1) * TOK)
                sub = b * PER + p
                top = tops[at, rows, :1]
                others = []
                for place in range(parts):
                    column = [
                        jnp.sum(jnp.where(eye, stat_in[place, h, n : n + 1], 0.0), axis=1, keepdims=True)
                        for n in (sub, XS + sub)
                    ]
                    others.append(column)
                peak = top
                for other_top, _ in others:
                    peak = jnp.maximum(peak, other_top)
                keep = jnp.exp2((top - peak) * EXPO)
                total = totals[at, rows, :1] * keep
                acc = accs[at, rows, :] * keep
                for place, (other_top, other_total) in enumerate(others):
                    w = jnp.exp2((other_top - peak) * EXPO) * other_total
                    total = total + w
                    acc = acc + part_in[place, h, sub].astype(jnp.float32) * w
                accs[at, rows, :] = acc / total

    def out_copy(h, t):
        return pltpu.make_async_remote_copy(
            mixed.at[h, t], out_ref.at[:, cols(x * LOCAL + h)], x_send.at[OUT, h, t], x_recv.at[OUT, h, x],
            device_id={"dp": dp, "ctx": row * XS + t}, device_id_type=MESH,
        )

    def own_out(h):
        return pltpu.make_async_copy(mixed.at[h, x], out_ref.at[:, cols(x * LOCAL + h)], own_sem.at[OUT, h])

    def emit(h):
        @pl.when(row == 2)
        def _():
            z_copy(ZO2, h).wait_recv()
            z_copy(ZS2, h).wait_recv()
            merge(h, 1)

        @pl.when(row == 3)
        def _():
            z_copy(ZO3, h).wait_recv()
            z_copy(ZS3, h).wait_recv()
            z_copy(ZO3B, h).wait_recv()
            z_copy(ZS3B, h).wait_recv()
            merge(h, 2)

        @pl.when((h != y) | inner)
        def _():
            there = cross.at[h]
            pltpu.make_async_remote_copy(
                there, there, back_send.at[0, 0], back_recv.at[h],
                device_id={"dp": side + 2 * h + core, "ctx": cross_row * XS + x}, device_id_type=MESH,
            ).wait_recv()

        @pl.when((h == y) & edge)
        def _():
            own_back().wait()

        self_out = accs[pl.ds(h * QB, QB)].astype(jnp.bfloat16).astype(jnp.float32).reshape(XS, TOK, HD)
        mixed[h] = (self_out + cross[h].astype(jnp.float32)).astype(jnp.bfloat16)
        for k in (1, 3, 2):
            out_copy(h, x_at(k)).start()
        own_out(h).start()

    def own_and_emit(h):
        own_others(h)
        emit(h)

    loop(0, LOCAL, own_and_emit)

    @pl.when(edge)
    def _():
        for kind in range(2):
            far_copy(kind).wait_send()
            for far in range(2):
                for k in range(1, 4):
                    y_copy(kind, far, k).wait_send()
                for k in range(4):
                    core_pass(kind, far, k).wait_send()
        for k in range(1, 4):
            back_copy(0, k).wait_send()
        for k in range(4):
            back_copy(1, k).wait_send()

    def finish_plane(k):
        idx_copy(k).wait_send()
        qc_copy(k).wait_send()

    loop(first_plane, 4 * XS, finish_plane)
    def finish(h):
        for k in range(1, XS):
            peer = x_at(k)
            for kind in (KS, VS, QS):
                x_copy(kind, h, peer).wait_send()
        for at, kinds in enumerate(((ZK, ZV), (ZO2, ZS2, ZO3, ZS3), (ZQ2, ZO3B, ZS3B), (ZQ3, ZQ3B))):

            @pl.when(row == at)
            def _():
                for kind in kinds:
                    z_copy(kind, h).wait_send()

    def finish_out(h):
        own_out(h).wait()
        for k in range(1, XS):
            peer = x_at(k)
            out_copy(h, peer).wait_send()
            pltpu.make_async_remote_copy(
                mixed.at[h, peer], out_ref.at[:, cols(peer * LOCAL + h)], x_send.at[OUT, h, peer], x_recv.at[OUT, h, peer],
                device_id={"dp": dp, "ctx": row * XS + peer}, device_id_type=MESH,
            ).wait_recv()

    loop(0, LOCAL, finish)
    loop(0, LOCAL, finish_out)


def shards(q_self, k_self, v_self, q_cross, db_keys, db_values, nb_shard, nb_row):
    anywhere = pl.BlockSpec(memory_space=pl.ANY)
    scalars = pl.BlockSpec(memory_space=pltpu.SMEM)
    heads = pltpu.VMEM((LOCAL, XS, TOK, HD), jnp.bfloat16)
    database = pltpu.VMEM((N_DP * DB_DEV, NLEN, HD), jnp.bfloat16)
    shard = pltpu.VMEM((DB_DEV, NLEN, WIDE), jnp.bfloat16)
    state = pltpu.VMEM((LOCAL * QB, ROWS, HD), jnp.float32)
    parts = pltpu.VMEM((2, LOCAL, XS, TOK, HD), jnp.bfloat16)
    stats = pltpu.VMEM((2, LOCAL, 8, 128), jnp.float32)
    dma = pltpu.SemaphoreType.DMA
    out = pl.pallas_call(
        kernel,
        out_shape=jax.ShapeDtypeStruct((TOK, HEADS * HD), jnp.bfloat16),
        in_specs=[anywhere] * 6 + [scalars] * 2,
        out_specs=anywhere,
        scratch_shapes=[
            heads, heads, heads, parts, heads, heads, heads, heads, database, database,
            pltpu.VMEM((2, 4, XS, 8, 128), jnp.int32),
            pltpu.SMEM((2, 4, XS, 8, 128), jnp.int32),
            heads,
            pltpu.VMEM((3, 2 * QB, ROWS, ROWS), jnp.float32),
            state, state, state,
            parts, stats, parts, stats, heads, parts, shard, shard,
            dma((5, LOCAL, XS)), dma((5, LOCAL, XS)), dma((4 * XS,)), dma((2, 4, XS)), dma((4 * XS,)), dma((2, 4, XS)),
            dma((2, 4)), dma((4,)), dma((11, LOCAL)), dma((11, LOCAL)),
            dma((2,)), dma((2,)), dma((2, 2, 4)), dma((2, 2, 4)), dma((2, N_DP)), dma((5, LOCAL)), dma((4,)), dma,
            pltpu.SemaphoreType.REGULAR,
        ],
        compiler_params=pltpu.CompilerParams(
            collective_id=0, has_side_effects=True, vmem_limit_bytes=60 * 1024 * 1024
        ),
    )(q_self[0], k_self[0], v_self[0], q_cross[0], db_keys, db_values, nb_shard, nb_row)
    return out[None]


def solution(mesh):
    return jax.shard_map(
        shards,
        mesh=mesh,
        in_specs=(
            P("dp", "ctx", None),
            P("dp", "ctx", None),
            P("dp", "ctx", None),
            P("dp", "ctx", None),
            P("dp", None, None),
            P("dp", None, None),
            P("dp", "ctx", None),
            P("dp", "ctx", None),
        ),
        out_specs=P("dp", "ctx", None),
        check_vma=False,
    )
```

profile of v0, /device:TPU:32, one launch (start us, length us, event | category | flops | bytes accessed | tf_op | source)
XLA Modules:
  0.0 64.7 jit_solution(13809404865605301202)
XLA Ops:
  0.0 62.8 %shard_map.82 = bf16[128,2048]{1,0:T(8,128)(2,1)} custom-call(bf16[128,2048]{1,0:T(8,128)(2,1)} %bitcast.6, bf16[128,2048]{1,0:T(8,128)(2,1)} %bitcast.7, bf16[128,2048]{1,0:T(8,128)(2,1)} %bitcast.8, bf16[128,2048]{1,0:T(8,128)(2,1)} %bitcast.9, bf16[2,128,2048]{2,1,0:T(8,128)(2,1)} %kd_ref.1, bf16[2,128,2048]{2,1,0:T(8,128)(2,1)} %vd_ref.1, ...), custom_call_target="tpu_custom_call" | custom-call | tf_op jit(solution)/shard_map/pallas_call | solution.py:657
  62.8 1.9 %copy.10 = bf16[1,128,2048]{2,1,0:T(8,128)(2,1)} copy(bf16[1,128,2048]{2,1,0:T(8,128)(2,1)} %bitcast.5) | data formatting | bytes 1048576
where the time goes:
time: 65.9 us; the launch traced here: 64.7 us
  Pallas kernels  62.8 us (95%)
  local copies, waits for them, and re-layouts  1.88 us (3%)
    pallas_call x1, Pallas kernels, shards(): pl.pallas_call(kernel, out_shape=jax.ShapeDtypeStruct((TOK, HEADS * HD),...  62.8 us
    unnamed x1, local copies, waits for them, and re-layouts  1.88 us

commit v1 on v0

--- a/solution.py
+++ b/solution.py
@@ -16,7 +16,6 @@
 HALF = 8
 XS = 4
 LOCAL = HEADS // XS
-WIDE = LOCAL * HD
 ROWS = 256
 PER = ROWS // TOK
 QB = XS // PER
@@ -35,9 +34,9 @@
 def kernel(
     qs_ref, ks_ref, vs_ref, qc_ref, kd_ref, vd_ref, shard_ref, row_ref, out_ref,
     qs, ks, vs, qc, k0, v0, q2, q3, kd, vd, idx, idx_s, cross, scores, tops, totals, accs,
-    part_out, stat_out, part_in, stat_in, mixed, cross_out, kf, vf,
+    part_out, stat_out, part_in, stat_in, mixed, cross_out,
     x_send, x_recv, qc_send, qc_recv, idx_send, idx_recv, back_send, back_recv, z_send, z_recv,
-    far_send, far_recv, y_send, core_send, db_recv, own_sem, db_own, number_sem, ready,
+    y_send, core_send, db_recv, own_sem, db_own, number_sem, ready,
 ):
     dp = lax.axis_index("dp")
     me = lax.axis_index("ctx")
@@ -49,7 +48,6 @@
     y = near // 2
     core = lax.rem(near, 2)
     other_core = dp + 1 - 2 * core
-    far_dp = away + near
     far_ctx = (3 - row) * XS + x
     edge = (row == 0) | (row == 3)
     first_side = dp < HALF
@@ -97,7 +95,8 @@
 
     @pl.when(edge & first_side)
     def _():
-        greet(far_dp, far_ctx)
+        for k in range(4):
+            greet(y_at(away, k), far_ctx)
 
     lane = lax.broadcasted_iota(jnp.int32, (8, 128), 1)
     tile = jnp.zeros((8, 128), jnp.int32)
@@ -108,8 +107,7 @@
     idx[cross_part, y, x] = tile
 
     arrays = {KS: (ks_ref, ks), VS: (vs_ref, vs), QS: (qs_ref, qs)}
-    blocks = ((kd_ref, kd, kf), (vd_ref, vd, vf))
-    wide = pl.ds(pl.multiple_of(x * WIDE, WIDE), WIDE)
+    blocks = ((kd_ref, kd), (vd_ref, vd))
     head = x * LOCAL + y
 
     def own_copy(kind, h):
@@ -120,12 +118,8 @@
         return pltpu.make_async_copy(qc_ref.at[:, cols(head)], qc.at[0, y, x], own_sem.at[QC, 0])
 
     def own_db(kind):
-        arg, buf, far = blocks[kind]
+        arg, buf = blocks[kind]
         return pltpu.make_async_copy(arg.at[:, :, cols(head)], buf.at[pl.ds(dp * DB_DEV, DB_DEV)], db_own.at[kind])
-
-    def own_far(kind):
-        arg, buf, far = blocks[kind]
-        return pltpu.make_async_copy(far.at[:, :, cols(y)], buf.at[pl.ds(far_dp * DB_DEV, DB_DEV)], db_own.at[2 + kind])
 
     def start_own(h):
         for kind in (KS, VS, QS):
@@ -139,39 +133,31 @@
         for kind in range(2):
             own_db(kind).start()
 
-    pl.semaphore_wait(barrier, 21 + jnp.where(edge, 13, 0) + jnp.where(edge & (dp >= HALF), 1, 0))
+    pl.semaphore_wait(barrier, 21 + jnp.where(edge, 13, 0) + jnp.where(edge & (dp >= HALF), 4, 0))
 
     @pl.when(edge & (dp >= HALF))
     def _():
-        pl.semaphore_signal(ready, inc=1, device_id={"dp": far_dp, "ctx": far_ctx}, device_id_type=MESH)
-
-    def far_copy(kind):
-        arg, buf, far = blocks[kind]
-        return pltpu.make_async_remote_copy(
-            arg.at[:, :, wide], far, far_send.at[kind], far_recv.at[kind],
-            device_id={"dp": far_dp, "ctx": far_ctx}, device_id_type=MESH,
-        )
-
-    def shard_copy(kind, shard, src, send, target):
+        for k in range(4):
+            pl.semaphore_signal(ready, inc=1, device_id={"dp": y_at(away, k), "ctx": far_ctx}, device_id_type=MESH)
+
+    def shard_copy(kind, shard, src, send, target, target_ctx):
         part = blocks[kind][1].at[pl.ds(shard * DB_DEV, DB_DEV)]
         return pltpu.make_async_remote_copy(
             part if src is None else src, part, send, db_recv.at[kind, shard],
-            device_id={"dp": target, "ctx": me}, device_id_type=MESH,
+            device_id={"dp": target, "ctx": target_ctx}, device_id_type=MESH,
         )
 
     def y_copy(kind, far, k):
-        to_y = lax.rem(y + k, 4)
-        src = blocks[kind][2].at[:, :, cols(to_y)] if far else blocks[kind][0].at[:, :, cols(x * LOCAL + to_y)]
-        return shard_copy(kind, far_dp if far else dp, src, y_send.at[kind, far, k], y_at(side, k))
+        src = blocks[kind][0].at[:, :, cols(x * LOCAL + lax.rem(y + k, 4))]
+        target = y_at(away if far else side, k)
+        return shard_copy(kind, dp, src, y_send.at[kind, far, k], target, far_ctx if far else me)
 
     def core_pass(kind, far, k):
-        src = None
-        if k == 0:
-            src = blocks[kind][2].at[:, :, cols(y)] if far else blocks[kind][0].at[:, :, cols(head)]
-        return shard_copy(kind, y_at(away if far else side, k), src, core_send.at[kind, far, k], other_core)
+        src = blocks[kind][0].at[:, :, cols(head)] if (far, k) == (0, 0) else None
+        return shard_copy(kind, y_at(away if far else side, k), src, core_send.at[kind, far, k], other_core, me)
 
     def wait_shard(kind, shard):
-        shard_copy(kind, shard, None, far_send.at[kind], other_core).wait_recv()
+        shard_copy(kind, shard, None, y_send.at[kind, 0, 0], other_core, me).wait_recv()
 
     def qc_copy(k):
         to_y, to_x = plane(k)
@@ -254,14 +240,16 @@
         @pl.when(dp >= HALF)
         def _():
             for kind in range(2):
-                far_copy(kind).start()
+                for k in range(4):
+                    y_copy(kind, 1, k).start()
 
     def start_far_second():
         @pl.when(first_side)
         def _():
-            pl.semaphore_wait(ready, 1)
+            pl.semaphore_wait(ready, 4)
             for kind in range(2):
-                far_copy(kind).start()
+                for k in range(4):
+                    y_copy(kind, 1, k).start()
 
     @pl.when(row == 0)
     def _():
@@ -331,18 +319,10 @@
             z_copy(ZQ3, h).start()
             z_copy(ZQ3B, h).start()
 
-    def far_stage():
-        for kind in range(2):
-            far_copy(kind).wait_recv()
-            for k in (1, 3, 2):
-                y_copy(kind, 1, k).start()
-            core_pass(kind, 1, 0).start()
-            own_far(kind).start()
-
     def core_stage():
         for far in range(2):
             for kind in range(2):
-                for k in (1, 3, 2):
+                for k in (0, 1, 3, 2)[1 - far :]:
                     wait_shard(kind, y_at(away if far else side, k))
                     core_pass(kind, far, k).start()
 
@@ -486,7 +466,6 @@
         own_qc().wait()
         for kind in range(2):
             own_db(kind).wait()
-            own_far(kind).wait()
 
         def wait_other_core(k):
             for kind in range(2):
@@ -506,17 +485,11 @@
 
     @pl.when(row == 0)
     def _():
-        relay(0)
-        relay(1)
-        far_stage()
-        relay(2)
-        relay(3)
+        loop(0, LOCAL, relay)
 
     @pl.when(row >= 2)
     def _():
         loop(0, LOCAL, relay)
-
-    pl.when(row == 3)(far_stage)
 
     @pl.when(edge)
     def _():
@@ -602,9 +575,8 @@
     @pl.when(edge)
     def _():
         for kind in range(2):
-            far_copy(kind).wait_send()
             for far in range(2):
-                for k in range(1, 4):
+                for k in range(1 - far, 4):
                     y_copy(kind, far, k).wait_send()
                 for k in range(4):
                     core_pass(kind, far, k).wait_send()
@@ -649,7 +621,6 @@
     scalars = pl.BlockSpec(memory_space=pltpu.SMEM)
     heads = pltpu.VMEM((LOCAL, XS, TOK, HD), jnp.bfloat16)
     database = pltpu.VMEM((N_DP * DB_DEV, NLEN, HD), jnp.bfloat16)
-    shard = pltpu.VMEM((DB_DEV, NLEN, WIDE), jnp.bfloat16)
     state = pltpu.VMEM((LOCAL * QB, ROWS, HD), jnp.float32)
     parts = pltpu.VMEM((2, LOCAL, XS, TOK, HD), jnp.bfloat16)
     stats = pltpu.VMEM((2, LOCAL, 8, 128), jnp.float32)
@@ -666,10 +637,10 @@
             heads,
             pltpu.VMEM((3, 2 * QB, ROWS, ROWS), jnp.float32),
             state, state, state,
-            parts, stats, parts, stats, heads, parts, shard, shard,
+            parts, stats, parts, stats, heads, parts,
             dma((5, LOCAL, XS)), dma((5, LOCAL, XS)), dma((4 * XS,)), dma((2, 4, XS)), dma((4 * XS,)), dma((2, 4, XS)),
             dma((2, 4)), dma((4,)), dma((11, LOCAL)), dma((11, LOCAL)),
-            dma((2,)), dma((2,)), dma((2, 2, 4)), dma((2, 2, 4)), dma((2, N_DP)), dma((5, LOCAL)), dma((4,)), dma,
+            dma((2, 2, 4)), dma((2, 2, 4)), dma((2, N_DP)), dma((5, LOCAL)), dma((2,)), dma,
             pltpu.SemaphoreType.REGULAR,
         ],
         compiler_params=pltpu.CompilerParams(

time: 65.9 us -> 62.7 us (0.951); the launches traced: 64.7 us -> 62.6 us
  Pallas kernels: 62.8 us -> 60.7 us
    pallas_call x1, Pallas kernels: 62.8 us -> 60.7 us  [shards(): pl.pallas_call(kernel, out_shape=jax.ShapeDtypeStruct((TOK, HEADS * HD),...]
where the time goes in v1:
time: 62.7 us; the launch traced here: 62.6 us
  Pallas kernels  60.7 us (97%)
  local copies, waits for them, and re-layouts  1.88 us (3%)
    pallas_call x1, Pallas kernels, shards(): pl.pallas_call(kernel, out_shape=jax.ShapeDtypeStruct((TOK, HEADS * HD),...  60.7 us
    unnamed x1, local copies, waits for them, and re-layouts  1.88 us

profile of v1, /device:TPU:32, one launch (start us, length us, event | category | flops | bytes accessed | tf_op | source)
XLA Modules:
  0.0 62.6 jit_solution(966370323716158942)
XLA Ops:
  0.0 60.7 %shard_map.82 = bf16[128,2048]{1,0:T(8,128)(2,1)} custom-call(bf16[128,2048]{1,0:T(8,128)(2,1)} %bitcast.6, bf16[128,2048]{1,0:T(8,128)(2,1)} %bitcast.7, bf16[128,2048]{1,0:T(8,128)(2,1)} %bitcast.8, bf16[128,2048]{1,0:T(8,128)(2,1)} %bitcast.9, bf16[2,128,2048]{2,1,0:T(8,128)(2,1)} %kd_ref.1, bf16[2,128,2048]{2,1,0:T(8,128)(2,1)} %vd_ref.1, ...), custom_call_target="tpu_custom_call" | custom-call | tf_op jit(solution)/shard_map/pallas_call | solution.py:628
  60.7 1.9 %copy.10 = bf16[1,128,2048]{2,1,0:T(8,128)(2,1)} copy(bf16[1,128,2048]{2,1,0:T(8,128)(2,1)} %bitcast.5) | data formatting | bytes 1048576

commit v2 on v1

--- a/solution.py
+++ b/solution.py
@@ -251,36 +251,6 @@
                 for k in range(4):
                     y_copy(kind, 1, k).start()
 
-    @pl.when(row == 0)
-    def _():
-        start_far_first()
-        start_x((KS, VS))
-        start_near()
-        start_plane()
-        start_far_second()
-        start_x((QS,))
-
-    @pl.when(row == 1)
-    def _():
-        start_plane()
-        start_x((KS, VS))
-        start_x((QS,))
-
-    @pl.when(row == 2)
-    def _():
-        start_x((QS,))
-        start_plane()
-        start_x((KS, VS))
-
-    @pl.when(row == 3)
-    def _():
-        start_far_first()
-        start_x((QS,))
-        start_near()
-        start_plane()
-        start_far_second()
-        start_x((KS, VS))
-
     def z_copy(kind, h):
         src, dst, to = {
             ZK: (ks.at[h], k0.at[h], 1),
@@ -317,7 +287,6 @@
         def _():
             arrived(QS, h)
             z_copy(ZQ3, h).start()
-            z_copy(ZQ3B, h).start()
 
     def core_stage():
         for far in range(2):
@@ -485,11 +454,38 @@
 
     @pl.when(row == 0)
     def _():
+        start_far_first()
+        start_x((KS, VS))
+        start_near()
+        relay(0)
+        start_far_second()
+        start_plane()
+        loop(1, LOCAL, relay)
+        start_x((QS,))
+
+    @pl.when(row == 1)
+    def _():
+        start_plane()
+        start_x((KS, VS))
+        start_x((QS,))
+
+    @pl.when(row == 2)
+    def _():
+        start_x((QS,))
         loop(0, LOCAL, relay)
-
-    @pl.when(row >= 2)
-    def _():
+        start_plane()
+        start_x((KS, VS))
+
+    @pl.when(row == 3)
+    def _():
+        start_far_first()
+        start_x((QS,))
+        start_near()
         loop(0, LOCAL, relay)
+        start_far_second()
+        start_plane()
+        loop(0, LOCAL, lambda h: z_copy(ZQ3B, h).start())
+        start_x((KS, VS))
 
     @pl.when(edge)
     def _():

time: 62.7 us -> 64.4 us (1.027)
  the two profiles are of different devices: /device:TPU:32 before, /device:TPU:224 now
where the time goes in v2:
time: 64.4 us; the launch traced here: 64.3 us
  Pallas kernels  62.4 us (97%)
  local copies, waits for them, and re-layouts  1.88 us (3%)
    pallas_call x1, Pallas kernels, shards(): pl.pallas_call(kernel, out_shape=jax.ShapeDtypeStruct((TOK, HEADS * HD),...  62.4 us
    unnamed x1, local copies, waits for them, and re-layouts  1.88 us

profile of v2, /device:TPU:224, one launch (start us, length us, event | category | flops | bytes accessed | tf_op | source)
XLA Modules:
  0.0 64.3 jit_solution(13005848983700220178)
XLA Ops:
  0.0 62.4 %shard_map.82 = bf16[128,2048]{1,0:T(8,128)(2,1)} custom-call(bf16[128,2048]{1,0:T(8,128)(2,1)} %bitcast.6, bf16[128,2048]{1,0:T(8,128)(2,1)} %bitcast.7, bf16[128,2048]{1,0:T(8,128)(2,1)} %bitcast.8, bf16[128,2048]{1,0:T(8,128)(2,1)} %bitcast.9, bf16[2,128,2048]{2,1,0:T(8,128)(2,1)} %kd_ref.1, bf16[2,128,2048]{2,1,0:T(8,128)(2,1)} %vd_ref.1, ...), custom_call_target="tpu_custom_call" | custom-call | tf_op jit(solution)/shard_map/pallas_call | solution.py:624
  62.4 1.9 %copy.10 = bf16[1,128,2048]{2,1,0:T(8,128)(2,1)} copy(bf16[1,128,2048]{2,1,0:T(8,128)(2,1)} %bitcast.5) | data formatting | bytes 1048576

commit v3 on v1

--- a/solution.py
+++ b/solution.py
@@ -319,12 +319,11 @@
             z_copy(ZQ3, h).start()
             z_copy(ZQ3B, h).start()
 
-    def core_stage():
-        for far in range(2):
-            for kind in range(2):
-                for k in (0, 1, 3, 2)[1 - far :]:
-                    wait_shard(kind, y_at(away if far else side, k))
-                    core_pass(kind, far, k).start()
+    def core_stage(far):
+        for kind in range(2):
+            for k in (0, 1, 3, 2)[1 - far :]:
+                wait_shard(kind, y_at(away if far else side, k))
+                core_pass(kind, far, k).start()
 
     diagonal = lax.broadcasted_iota(jnp.int32, (ROWS, ROWS), 0) >= lax.broadcasted_iota(jnp.int32, (ROWS, ROWS), 1)
     eye = lax.broadcasted_iota(jnp.int32, (TOK, TOK), 0) == lax.broadcasted_iota(jnp.int32, (TOK, TOK), 1)
@@ -433,12 +432,12 @@
             arrived(VS, h)
             attend(h, own_rows(h, [], False))
 
-    def cross_document(part, k):
-        doc = lax.rem(y + k, 4)
-        groups = [(t, g) for t in range(XS) for g in range(TOK // GROUP)]
-        picks = [[idx_s[part, doc, t, 0, g * NEIGH + n] for n in range(NEIGH)] for t, g in groups]
+    def cross_documents(part, pairs):
+        docs = [lax.rem(y + 3 - 2 * pairs - n, 4) for n in range(2)]
+        groups = [(doc, t, g) for doc in docs for t in range(XS) for g in range(TOK // GROUP)]
+        picks = [[idx_s[part, doc, t, 0, g * NEIGH + n] for n in range(NEIGH)] for doc, t, g in groups]
         s = []
-        for (t, g), pick in zip(groups, picks):
+        for (doc, t, g), pick in zip(groups, picks):
             keys = jnp.concatenate([kd[block] for block in pick], axis=0)
             q = qc[part, doc, t, pl.ds(g * GROUP, GROUP), :]
             s.append(lax.dot_general(q, keys, NT, preferred_element_type=jnp.float32))
@@ -449,9 +448,13 @@
         for one, pick in zip(w, picks):
             values = jnp.concatenate([vd[block] for block in pick], axis=0)
             o.append(lax.dot_general(one.astype(jnp.bfloat16), values, NN, preferred_element_type=jnp.float32))
-        for (t, g), one, whole in zip(groups, o, total):
+        for (doc, t, g), one, whole in zip(groups, o, total):
             cross_out[part, doc, t, pl.ds(g * GROUP, GROUP), :] = (one / whole).astype(jnp.bfloat16)
 
+        back_copy(part, 3 - 2 * pairs).start()
+        send_back(part, 2 - 2 * pairs)
+
+    def send_back(part, k):
         here = (part == 0) & (k == 0)
 
         @pl.when(jnp.logical_not(here))
@@ -479,39 +482,38 @@
             numbers = pltpu.make_async_copy(idx.at[part], idx_s.at[part], number_sem)
             numbers.start()
             numbers.wait()
-            loop(0, 4, lambda k: cross_document(part, 3 - k))
+            loop(0, 2, lambda pairs: cross_documents(part, pairs))
 
         loop(0, 2, cross_row_of)
 
     @pl.when(row == 0)
     def _():
+        loop(0, 2, relay)
+        core_stage(0)
+        loop(2, LOCAL, relay)
+
+    @pl.when(row >= 2)
+    def _():
         loop(0, LOCAL, relay)
 
-    @pl.when(row >= 2)
-    def _():
-        loop(0, LOCAL, relay)
+    pl.when(row == 3)(lambda: core_stage(0))
 
     @pl.when(edge)
     def _():
-        core_stage()
+        core_stage(1)
         cross_stage()
 
     loop(0, LOCAL, between)
 
     def merge(h, parts):
+        columns = [jnp.transpose(stat_in[place, h]) for place in range(parts)]
         for b in range(QB):
             at = h * QB + b
             for p in range(PER):
                 rows = slice(p * TOK, (p + 1) * TOK)
                 sub = b * PER + p
                 top = tops[at, rows, :1]
-                others = []
-                for place in range(parts):
-                    column = [
-                        jnp.sum(jnp.where(eye, stat_in[place, h, n : n + 1], 0.0), axis=1, keepdims=True)
-                        for n in (sub, XS + sub)
-                    ]
-                    others.append(column)
+                others = [(one[:, sub : sub + 1], one[:, XS + sub : XS + sub + 1]) for one in columns]
                 peak = top
                 for other_top, _ in others:
                     peak = jnp.maximum(peak, other_top)

time: 62.7 us -> 64.2 us (1.024)
  Pallas kernels: 60.7 us -> 62.2 us
    pallas_call x1, Pallas kernels: 60.7 us -> 62.2 us  [shards(): pl.pallas_call(kernel, out_shape=jax.ShapeDtypeStruct((TOK, HEADS * HD),...]
where the time goes in v3:
time: 64.2 us; the launch traced here: 64.1 us
  Pallas kernels  62.2 us (97%)
  local copies, waits for them, and re-layouts  1.88 us (3%)
    pallas_call x1, Pallas kernels, shards(): pl.pallas_call(kernel, out_shape=jax.ShapeDtypeStruct((TOK, HEADS * HD),...  62.2 us
    unnamed x1, local copies, waits for them, and re-layouts  1.88 us

profile of v3, /device:TPU:32, one launch (start us, length us, event | category | flops | bytes accessed | tf_op | source)
XLA Modules:
  0.0 64.1 jit_solution(1256679777176995223)
XLA Ops:
  0.0 62.2 %shard_map.82 = bf16[128,2048]{1,0:T(8,128)(2,1)} custom-call(bf16[128,2048]{1,0:T(8,128)(2,1)} %bitcast.6, bf16[128,2048]{1,0:T(8,128)(2,1)} %bitcast.7, bf16[128,2048]{1,0:T(8,128)(2,1)} %bitcast.8, bf16[128,2048]{1,0:T(8,128)(2,1)} %bitcast.9, bf16[2,128,2048]{2,1,0:T(8,128)(2,1)} %kd_ref.1, bf16[2,128,2048]{2,1,0:T(8,128)(2,1)} %vd_ref.1, ...), custom_call_target="tpu_custom_call" | custom-call | tf_op jit(solution)/shard_map/pallas_call | solution.py:630
  62.2 1.9 %copy.10 = bf16[1,128,2048]{2,1,0:T(8,128)(2,1)} copy(bf16[1,128,2048]{2,1,0:T(8,128)(2,1)} %bitcast.5) | data formatting | bytes 1048576

commit v4 on v1

--- a/solution.py
+++ b/solution.py
@@ -644,7 +644,7 @@
             pltpu.SemaphoreType.REGULAR,
         ],
         compiler_params=pltpu.CompilerParams(
-            collective_id=0, has_side_effects=True, vmem_limit_bytes=60 * 1024 * 1024
+            collective_id=0, has_side_effects=True, vmem_limit_bytes=53 * 1024 * 1024
         ),
     )(q_self[0], k_self[0], v_self[0], q_cross[0], db_keys, db_values, nb_shard, nb_row)
     return out[None]

time: 62.7 us -> 62.1 us (level)
    unnamed x1 -> x5, local copies, waits for them, and re-layouts: 1.88 us -> 1.49 us
where the time goes in v4:
time: 62.1 us; the launch traced here: 62 us
  Pallas kernels  60.5 us (97%)
  local copies, waits for them, and re-layouts  1.49 us (2%)
    pallas_call x1, Pallas kernels, shards(): pl.pallas_call(kernel, out_shape=jax.ShapeDtypeStruct((TOK, HEADS * HD),...  60.5 us
    unnamed x5, local copies, waits for them, and re-layouts  1.49 us

profile of v4, /device:TPU:32, one launch (start us, length us, event | category | flops | bytes accessed | tf_op | source)
XLA Modules:
  0.0 62.0 jit_solution(16134958744272732586)
XLA Ops:
  0.0 0.0 copy-start.1
  0.0 0.0 copy-start
  0.0 0.7 %copy-done.1 = s32[1,2,2]{2,1,0:T(2,128)S(1)} copy-done((s32[1,2,2]{2,1,0:T(2,128)S(1)}, s32[1,2,2]{2,1,0:T(2,128)}, u32[]{:S(2)}) %copy-start.1) | copy-done | bytes 40
  0.7 0.0 copy-done
  0.7 60.5 %shard_map.82 = bf16[128,2048]{1,0:T(8,128)(2,1)S(1)} custom-call(bf16[128,2048]{1,0:T(8,128)(2,1)} %bitcast.6, bf16[128,2048]{1,0:T(8,128)(2,1)} %bitcast.7, bf16[128,2048]{1,0:T(8,128)(2,1)} %bitcast.8, bf16[128,2048]{1,0:T(8,128)(2,1)} %bitcast.9, bf16[2,128,2048]{2,1,0:T(8,128)(2,1)} %kd_ref.1, bf16[2,128,2048]{2,1,0:T(8,128)(2,1)} %vd_ref.1, ...), custom_call_target="tpu_custom_call" | custom-call | tf_op jit(solution)/shard_map/pallas_call | solution.py:628
  61.2 0.8 %copy.10 = bf16[1,128,2048]{2,1,0:T(8,128)(2,1)} copy(bf16[1,128,2048]{2,1,0:T(8,128)(2,1)S(1)} %bitcast.5) | data formatting | bytes 1048576
Async XLA Ops:
  0.0 0.7 %copy-start.1 = (s32[1,2,2]{2,1,0:T(2,128)S(1)}, s32[1,2,2]{2,1,0:T(2,128)}, u32[]{:S(2)}) copy-start(s32[1,2,2]{2,1,0:T(2,128)} %row_ref.1) | copy-start | bytes 52
  0.0 0.7 %copy-start = (s32[1,2,2]{2,1,0:T(2,128)S(1)}, s32[1,2,2]{2,1,0:T(2,128)}, u32[]{:S(2)}) copy-start(s32[1,2,2]{2,1,0:T(2,128)} %shard_ref.1) | copy-start | bytes 52
